TPU v7x, 32 devices: a whole 2x2x4 slice. The times are simulated.
32 devices in a mesh: jobs: 2 (over y), gr: 4 (over x, core), gc: 4 (over z).
Axes of the slice: x: 2, y: 2, z: 4, core: 2. Of those that a mesh axis runs over, the one named last changes fastest.
Arguments:
- pair: bfloat16 [160, 80, 128], P(('jobs', 'gr'), 'gc'), parts along dimension 0, may hold values from -6 to 6
- mask: int32 [160], P('jobs'), parts along dimension 0, may hold values 0 or 1
- chain_ids: int32 [160], P('jobs'), parts along dimension 0, may hold values from 0 to 3, never falling along the last dimension, each value on 1 to 40 neighbouring positions
- attn_in: bfloat16 [2, 128, 512], replicated, may hold values from -0.5 to 0.5
- attn_out: bfloat16 [2, 128, 128], replicated, may hold values from -0.5 to 0.5
- bias_weight: bfloat16 [2, 128, 4], replicated, may hold values from -16 to 16
- chain_bias: float32 [2, 4], replicated, may hold values from -6 to 6
- trans_up: bfloat16 [128, 512], replicated, may hold values from -0.5 to 0.5
- trans_down: bfloat16 [512, 128], replicated, may hold values from -0.25 to 0.25
Outputs:
- result: bfloat16 [160, 80, 128], P(('jobs', 'gr'), 'gc'), parts along dimension 0
There are 2 independent parts, one for each index of `jobs`. A program takes and returns all parts, laid end to end along the dimension named above; an argument that names none is the same for every part. Nothing has to cross between parts.
All inputs are finite; a program needn't handle non-finite values.
Results may differ from a plain program's by a relative error of at most 0.008.
The roundings to bfloat16 on the way count: a program that leaves them out, or rounds other values in their place, can miss the bound.
Values may be sent and summed in bfloat16 or wider, within the bound.
A program may use at most 64 MiB of HBM per device.

v0:
```python
import jax
import jax.numpy as jnp
from jax import lax
from jax.sharding import PartitionSpec as P


def layer_norm(values):
    floats = values.astype(jnp.float32)
    center = jnp.mean(floats, axis=-1, keepdims=True)
    spread = jnp.mean((floats - center) ** 2, axis=-1, keepdims=True)
    return ((floats - center) * lax.rsqrt(spread + 1e-05)).astype(jnp.bfloat16)


def bias_terms(normed, weight, offset, chain_left, chain_right):
    first, second, width = normed.shape
    heads = weight.shape[1]
    terms = jnp.dot(normed.reshape(-1, width), weight, preferred_element_type=jnp.float32)
    same = (chain_left[:, None] == chain_right[None, :]).astype(jnp.float32)
    return terms.reshape(first, second, heads) + offset[None, None, :] * same[:, :, None]


def attention(rows, normed, in_w, out_w, bias_full, maskadd):
    count, length, width = rows.shape
    heads = bias_full.shape[0]
    head_width = width // heads
    scale = head_width ** (-0.5)
    proj = jnp.dot(normed.reshape(-1, width), in_w, preferred_element_type=jnp.float32)
    proj = proj.astype(jnp.bfloat16).reshape(count, length, 4 * width)

    def one_row(piece):
        query = piece[:, 0:width].reshape(length, heads, head_width)
        keys = piece[:, width : 2 * width].reshape(length, heads, head_width)
        vals = piece[:, 2 * width : 3 * width].reshape(length, heads, head_width)
        gate = piece[:, 3 * width :].astype(jnp.float32)
        scores = jnp.einsum("jhd,khd->hjk", query, keys, preferred_element_type=jnp.float32) * scale
        scores = scores + bias_full + maskadd[None, None, :]
        probs = jax.nn.softmax(scores, axis=-1).astype(jnp.bfloat16)
        mixed = jnp.einsum("hjk,khd->jhd", probs, vals, preferred_element_type=jnp.float32)
        return (jax.nn.sigmoid(gate) * mixed.reshape(length, width)).astype(jnp.bfloat16)

    gated = lax.map(one_row, proj)
    update = jnp.dot(gated.reshape(-1, width), out_w, preferred_element_type=jnp.float32)
    return (rows.astype(jnp.float32) + update.reshape(rows.shape)).astype(jnp.bfloat16)


def transition(rows, trans_up, trans_down):
    width = rows.shape[-1]
    normed = layer_norm(rows).reshape(-1, width)
    hidden = jax.nn.relu(jnp.dot(normed, trans_up, preferred_element_type=jnp.float32)).astype(
        jnp.bfloat16
    )
    update = jnp.dot(hidden, trans_down, preferred_element_type=jnp.float32)
    return (rows.astype(jnp.float32) + update.reshape(rows.shape)).astype(jnp.bfloat16)


def per_device(
    pair, mask, chain_ids, attn_in, attn_out, bias_weight, chain_bias, trans_up, trans_down
):
    across = lax.axis_size("gc")
    rows = lax.all_to_all(pair, "gc", split_axis=0, concat_axis=1, tiled=True)
    count = rows.shape[0]
    first_row = (lax.axis_index("gr") * across + lax.axis_index("gc")) * count
    maskadd = jnp.where(mask > 0, 0.0, -1000000000.0).astype(jnp.float32)
    own_chain = lax.dynamic_slice_in_dim(chain_ids, first_row, count)
    normed = layer_norm(rows)
    start_part = bias_terms(normed, bias_weight[0], chain_bias[0], own_chain, chain_ids)
    start_full = lax.all_gather(
        jnp.transpose(start_part, (2, 0, 1)), ("gr", "gc"), axis=1, tiled=True
    )
    rows = attention(rows, normed, attn_in[0], attn_out[0], start_full, maskadd)
    tile = lax.all_to_all(rows, "gc", split_axis=1, concat_axis=0, tiled=True)
    tile = transition(tile, trans_up, trans_down)
    tile_rows, tile_cols = (tile.shape[0], tile.shape[1])
    chain_rows = lax.dynamic_slice_in_dim(chain_ids, lax.axis_index("gr") * tile_rows, tile_rows)
    chain_cols = lax.dynamic_slice_in_dim(chain_ids, lax.axis_index("gc") * tile_cols, tile_cols)
    end_part = bias_terms(layer_norm(tile), bias_weight[1], chain_bias[1], chain_rows, chain_cols)
    end_part = lax.all_gather(jnp.transpose(end_part, (2, 1, 0)), "gc", axis=1, tiled=True)
    end_full = lax.all_gather(end_part, "gr", axis=2, tiled=True)
    columns = lax.all_to_all(
        jnp.transpose(tile, (1, 0, 2)), "gr", split_axis=0, concat_axis=1, tiled=True
    )
    columns = attention(columns, layer_norm(columns), attn_in[1], attn_out[1], end_full, maskadd)
    returned = lax.all_to_all(columns, "gr", split_axis=1, concat_axis=0, tiled=True)
    return jnp.transpose(returned, (1, 0, 2))


def solution(mesh):
    in_specs = (P(("jobs", "gr"), "gc", None), P("jobs"), P("jobs"), P(), P(), P(), P(), P(), P())
    out_specs = P(("jobs", "gr"), "gc", None)
    return jax.shard_map(
        per_device, mesh=mesh, in_specs=in_specs, out_specs=out_specs, check_vma=False
    )
```

profile of v0, /device:TPU:0, one launch (start us, length us, event | category | flops | bytes accessed | tf_op | source)
XLA Modules:
  0.0 99.6 jit_solution(12495822166500596514)
XLA Ops:
  0.0 6.4 %all-to-all-start = ((bf16[20,20,128]{2,1,0:T(8,128)(2,1)}), bf16[20,20,128]{2,1,0:T(8,128)(2,1)S(1)}, u32[]{:S(2)}, u32[]{:S(2)}) async-start(bf16[20,20,128]{2,1,0:T(8,128)(2,1)} %param.13), calls=%async_computation | async-start | bytes 245760 | tf_op jit(solution)/shard_map/all_to_all | solution.py:60
  6.5 0.7 copy-done.3
  7.3 0.6 copy-done.4
  7.9 0.6 copy-done.7
  8.6 3.8 %all-to-all-done = bf16[20,20,128]{2,1,0:T(8,128)(2,1)S(1)} async-done(((bf16[20,20,128]{2,1,0:T(8,128)(2,1)}), bf16[20,20,128]{2,1,0:T(8,128)(2,1)S(1)}, u32[]{:S(2)}, u32[]{:S(2)}) %all-to-all-start) | async-done | bytes 102432 | tf_op jit(solution)/shard_map/all_to_all | solution.py:60
  12.6 0.3 multiply_reduce_fusion.2
  13.2 0.6 copy-done.5
  14.0 31.1 %all_gather.9 = f32[4,80,80]{2,0,1:T(4,128)S(1)} all-gather(f32[4,5,80]{2,0,1:T(4,128)S(1)} %fusion.21), channel_id=1, replica_groups=mesh['jobs'=2,'gr'=4,'gc'=4] {'gr','gc'}, dimensions={1}, use_global_device_ids=true | all-gather | bytes 108800 | tf_op jit(solution)/shard_map/all_gather | solution.py:67
  45.2 0.2 convolution_convert_fusion.1
  45.5 3.4 %while.20 = (s32[]{:T(128)}, bf16[5,80,128]{1,2,0:T(8,128)(2,1)S(1)}, bf16[5,80,512]{2,1,0:T(8,128)(2,1)S(1)}, f32[4,80,80]{1,2,0:T(8,128)S(1)}, f32[80]{0:T(128)S(1)}, /*index=5*/s32[]{:T(128)}) while((s32[]{:T(128)}, bf16[5,80,128]{1,2,0:T(8,128)(2,1)S(1)}, bf16[5,80,512]{2,1,0:T(8,128)(2,1)S(1)}, f32[4,80,80]{1,2,0:T(8,128)S(1)}, ...), condition=%wide.region_5.6_spmd, body=%wide.region_2.5_spmd.sunk | while | flops 3543520 | bytes 1096589 | solution.py:41
  45.6 0.2 fusion.98
  46.3 0.2 fusion.98
  48.9 0.8 copy-done.2
  49.7 0.2 fusion.18
  49.9 0.7 copy.97
  50.6 3.3 %all-to-all-start.1 = ((bf16[5,80,128]{2,0,1:T(8,128)(2,1)}), bf16[5,80,128]{2,0,1:T(8,128)(2,1)S(1)}, u32[]{:S(2)}, u32[]{:S(2)}) async-start(bf16[5,80,128]{2,0,1:T(8,128)(2,1)} %copy.97), calls=%async_computation.1 | async-start | bytes 327680 | tf_op jit(solution)/shard_map/all_to_all | solution.py:71
  54.1 5.9 %all-to-all-done.1 = bf16[5,80,128]{2,0,1:T(8,128)(2,1)S(1)} async-done(((bf16[5,80,128]{2,0,1:T(8,128)(2,1)}), bf16[5,80,128]{2,0,1:T(8,128)(2,1)S(1)}, u32[]{:S(2)}, u32[]{:S(2)}) %all-to-all-start.1) | async-done | bytes 102432 | tf_op jit(solution)/shard_map/all_to_all | solution.py:71
  60.2 0.3 multiply_reduce_fusion.1
  60.7 0.8 copy-done.6
  61.5 0.6 convert_reduce_fusion
  62.1 0.2 fusion.26
  62.6 0.7 copy.103
  63.3 3.3 %all-to-all-start.2 = ((bf16[20,20,128]{2,1,0:T(8,128)(2,1)}), bf16[20,20,128]{2,1,0:T(8,128)(2,1)S(1)}, u32[]{:S(2)}, u32[]{:S(2)}) async-start(bf16[20,20,128]{2,1,0:T(8,128)(2,1)} %copy.103), calls=%async_computation.2 | async-start | bytes 245760 | tf_op jit(solution)/shard_map/all_to_all | solution.py:79
  66.6 0.3 fusion.20
  67.0 13.5 %all_gather.10 = f32[4,80,20]{2,0,1:T(4,128)S(1)} all-gather(f32[4,20,20]{2,0,1:T(4,128)S(1)} %copy.110), channel_id=1, replica_groups=mesh['jobs'=2,'gr'=4,'gc'=4] {'gc'}, dimensions={1}, use_global_device_ids=true | all-gather | bytes 32000 | tf_op jit(solution)/shard_map/all_gather | solution.py:77
  80.6 5.7 %all_gather.11 = f32[4,80,80]{1,0,2:T(4,128)S(1)} all-gather(f32[4,80,20]{1,0,2:T(4,128)S(1)} %copy.111), channel_id=1, replica_groups=mesh['jobs'=2,'gr'=4,'gc'=4] {'gr'}, dimensions={2}, use_global_device_ids=true | all-gather | bytes 128000 | tf_op jit(solution)/shard_map/all_gather | solution.py:78
  86.5 0.2 multiply_reduce_fusion
  87.1 0.2 convolution_convert_fusion
  87.3 3.4 %while.21 = (s32[]{:T(128)}, bf16[5,80,128]{1,2,0:T(8,128)(2,1)S(1)}, bf16[5,80,512]{2,1,0:T(8,128)(2,1)S(1)}, f32[4,80,80]{1,2,0:T(8,128)S(1)}, f32[80]{0:T(128)S(1)}, /*index=5*/s32[]{:T(128)}) while((s32[]{:T(128)}, bf16[5,80,128]{1,2,0:T(8,128)(2,1)S(1)}, bf16[5,80,512]{2,1,0:T(8,128)(2,1)S(1)}, f32[4,80,80]{1,2,0:T(8,128)S(1)}, ...), condition=%wide.region_15.16_spmd, body=%wide.region_12.15_spmd.sunk | while | flops 3543520 | bytes 1096589 | solution.py:41
  90.8 0.2 fusion.19
  91.1 7.9 %all_to_all.45 = bf16[5,80,128]{2,0,1:T(8,128)(2,1)S(1)} all-to-all(bf16[5,80,128]{2,0,1:T(8,128)(2,1)S(1)} %copy.115), channel_id=1, replica_groups=mesh['jobs'=2,'gr'=4,'gc'=4] {'gr'}, dimensions={1} | all-to-all | bytes 204800 | tf_op jit(solution)/shard_map/all_to_all | solution.py:83
  99.0 0.7 copy.118
  (128 shorter events, 8.4 us)
Async XLA Ops:
  0.0 60.7 %copy-start = (bf16[512,128]{1,0:T(8,128)(2,1)S(1)}, bf16[512,128]{1,0:T(8,128)(2,1)}, u32[]{:S(2)}) copy-start(bf16[512,128]{1,0:T(8,128)(2,1)} %param.21) | copy-start | bytes 393220
  0.0 12.4 %all-to-all-start = ((bf16[20,20,128]{2,1,0:T(8,128)(2,1)}), bf16[20,20,128]{2,1,0:T(8,128)(2,1)S(1)}, u32[]{:S(2)}, u32[]{:S(2)}) async-start(bf16[20,20,128]{2,1,0:T(8,128)(2,1)} %param.13), calls=%async_computation | async-start | bytes 245760 | tf_op jit(solution)/shard_map/all_to_all | solution.py:60
  6.5 0.7 copy-start.3
  7.2 0.7 copy-start.4
  7.9 0.7 copy-start.7
  13.2 0.7 copy-start.5
  14.0 31.2 %copy-start.1 = (bf16[2,128,512]{2,1,0:T(8,128)(2,1)S(1)}, bf16[2,128,512]{2,1,0:T(8,128)(2,1)}, u32[]{:S(2)}) copy-start(bf16[2,128,512]{2,1,0:T(8,128)(2,1)} %param.16) | copy-start | bytes 786436
  48.9 0.8 copy-start.2
  50.6 9.3 %all-to-all-start.1 = ((bf16[5,80,128]{2,0,1:T(8,128)(2,1)}), bf16[5,80,128]{2,0,1:T(8,128)(2,1)S(1)}, u32[]{:S(2)}, u32[]{:S(2)}) async-start(bf16[5,80,128]{2,0,1:T(8,128)(2,1)} %copy.97), calls=%async_computation.1 | async-start | bytes 327680 | tf_op jit(solution)/shard_map/all_to_all | solution.py:71
  60.6 0.9 copy-start.6
  63.3 23.1 %all-to-all-start.2 = ((bf16[20,20,128]{2,1,0:T(8,128)(2,1)}), bf16[20,20,128]{2,1,0:T(8,128)(2,1)S(1)}, u32[]{:S(2)}, u32[]{:S(2)}) async-start(bf16[20,20,128]{2,1,0:T(8,128)(2,1)} %copy.103), calls=%async_computation.2 | async-start | bytes 245760 | tf_op jit(solution)/shard_map/all_to_all | solution.py:79
where the time goes:
time: 100 us; the launch traced here: 99.6 us
  blocking collectives  58.1 us (58%)
  starting transfers between devices  13.1 us (13%)
  waiting for transfers between devices  9.75 us (10%)
  local copies, waits for them, and re-layouts  8.6 us (9%)
  matrix products  5.86 us (6%)
  other arithmetic  3.36 us (3%)
    all_gather x1, blocking collectives, per_device(): lax.all_gather(jnp.transpose(start_part, (2, 0, 1)), ('gr', 'gc'), axis=1...  31.1 us
    all_gather x1, blocking collectives, per_device(): lax.all_gather(jnp.transpose(end_part, (2, 1, 0)), 'gc', axis=1, tiled=True)  13.5 us
    all_to_all x1, blocking collectives, per_device(): lax.all_to_all(columns, 'gr', split_axis=1, concat_axis=0, tiled=True)  7.86 us
    all_to_all x1, starting transfers between devices, per_device(): rows = lax.all_to_all(pair, 'gc', split_axis=0, concat_axis=1, tiled=True)  6.45 us
    all_to_all x1, waiting for transfers between devices, per_device(): tile = lax.all_to_all(rows, 'gc', split_axis=1, concat_axis=0, tiled=True)  5.9 us
    all_gather x1, blocking collectives, per_device(): end_full = lax.all_gather(end_part, 'gr', axis=2, tiled=True)  5.69 us
    unnamed x16, local copies, waits for them, and re-layouts  4.15 us
    all_to_all x1, waiting for transfers between devices, per_device(): rows = lax.all_to_all(pair, 'gc', split_axis=0, concat_axis=1, tiled=True)  3.84 us
  transfers between devices with their start and end apart: 3, of which 2 were waited for; matrix products, arithmetic and copies ran while one was open for 1% of the time, Pallas kernels for 0%

commit v1 on v0

v1 whole, which is shorter than its diff:
```python
import functools

import jax
import jax.numpy as jnp
from jax import lax
from jax.experimental import pallas as pl
from jax.experimental.pallas import tpu as pltpu
from jax.sharding import PartitionSpec as P

F32 = jnp.float32
BF16 = jnp.bfloat16
MESH = pl.DeviceIdType.MESH
LANES = 128
PADDED = -3e38


def padded_size(size):
    width = 16
    while width < size:
        width *= 2
    return width


def layer_norm(floats):
    center = jnp.mean(floats, axis=-1, keepdims=True)
    moved = floats - center
    spread = jnp.mean(moved * moved, axis=-1, keepdims=True)
    return (moved * lax.rsqrt(spread + 1e-05)).astype(BF16)


def dot(left, right):
    return jnp.dot(left, right, preferred_element_type=F32)


def dot_t(left, right):
    return lax.dot_general(left, right, (((1,), (1,)), ((), ())), preferred_element_type=F32)


class Phase:
    def __init__(self, count, width, n_p, n_s, p_axis, s_axis, chunks):
        self.P, self.S, self.Sp = count, width, padded_size(width)
        self.n_p, self.n_s, self.p_axis, self.s_axis = n_p, n_s, p_axis, s_axis
        self.unit = min(count, width)
        self.chunks = chunks
        self.rows = count // chunks
        self.keys = n_s * self.Sp
        group = max(1, 640 // self.keys)
        while self.rows % group:
            group -= 1
        self.group = group

    def scratch(self, heads, width):
        return [
            pltpu.VMEM((self.P, self.Sp, width), F32),
            pltpu.VMEM((self.n_s, self.P, self.Sp, width), BF16),
            pltpu.VMEM((self.P // self.unit, 8, self.unit * self.Sp), F32),
            pltpu.VMEM((self.S // self.unit, self.n_s, 8, self.unit * self.Sp), F32),
            pltpu.VMEM((heads, self.Sp, self.keys), F32),
            pltpu.SemaphoreType.DMA((self.chunks, self.n_s)),
            pltpu.SemaphoreType.DMA((self.chunks, self.n_s)),
            pltpu.SemaphoreType.DMA((self.P // self.unit, self.n_p)),
            pltpu.SemaphoreType.DMA((self.S // self.unit, self.n_s)),
        ]

    def device(self, p_index, s_index):
        return {self.p_axis: p_index, self.s_axis: s_index}

    def send_rows(self, refs, chunk):
        x, buf, _, _, _, send, recv, _, _ = refs
        mine = lax.axis_index(self.s_axis)
        rows = pl.ds(chunk * self.rows, self.rows)
        buf[mine, rows] = layer_norm(x[rows])
        for step in range(1, self.n_s):
            peer = lax.rem(mine + step, self.n_s)
            pltpu.make_async_remote_copy(
                src_ref=buf.at[mine, rows],
                dst_ref=buf.at[mine, rows],
                send_sem=send.at[chunk, step],
                recv_sem=recv.at[chunk, mine],
                device_id=self.device(lax.axis_index(self.p_axis), peer),
                device_id_type=MESH,
            ).start()

    def wait_rows(self, refs, chunk):
        _, buf, _, _, _, _, recv, _, _ = refs
        mine = lax.axis_index(self.s_axis)
        rows = pl.ds(chunk * self.rows, self.rows)
        for step in range(1, self.n_s):
            peer = lax.rem(mine + step, self.n_s)
            spot = buf.at[peer, rows]
            pltpu.make_async_copy(spot, spot, recv.at[chunk, peer]).wait()

    def piece(self, k):
        start = lax.axis_index(self.p_axis) * self.P + k * self.unit
        return start // self.S, lax.rem(start, self.S) // self.unit

    def bias_copies(self, refs, begin):
        _, _, part, got, _, _, _, send, recv = refs
        mine_p, mine_s = lax.axis_index(self.p_axis), lax.axis_index(self.s_axis)
        for k in range(self.P // self.unit):
            target, slot = self.piece(k)
            for step in range(self.n_p):
                row = lax.rem(mine_p + step, self.n_p)
                copy = pltpu.make_async_remote_copy(
                    src_ref=part.at[k],
                    dst_ref=got.at[slot, mine_s],
                    send_sem=send.at[k, step],
                    recv_sem=recv.at[slot, mine_s],
                    device_id=self.device(row, target),
                    device_id_type=MESH,
                )
                act = copy.start if begin else copy.wait_send
                if step > 0:
                    act()
                    continue
                pl.when(target != mine_s)(act)
                if begin:

                    @pl.when(target == mine_s)
                    def _():
                        pltpu.make_async_copy(
                            part.at[k], got.at[slot, mine_s], recv.at[slot, mine_s]
                        ).start()

    def send_bias(self, refs, weight):
        _, buf, part, _, _, _, _, _, _ = refs
        mine = lax.axis_index(self.s_axis)
        for k in range(self.P // self.unit):
            own = buf[mine, k * self.unit : (k + 1) * self.unit]
            part[k] = dot_t(weight, own.reshape(self.unit * self.Sp, own.shape[-1]))[:8]
        self.bias_copies(refs, True)

    def finish_bias(self, refs, extra):
        _, _, _, got, bias, _, _, _, recv = refs
        bias[...] = extra[...]
        heads = bias.shape[0]
        share = max(1, LANES // self.Sp)
        for ks in range(self.S // self.unit):
            for b in range(self.n_s):
                spot = got.at[ks, b]
                pltpu.make_async_copy(spot, spot, recv.at[ks, b]).wait()
        lane = lax.broadcasted_iota(jnp.int32, (8, LANES), 1) // min(self.Sp, LANES)
        for ks in range(self.S // self.unit):
            for q in range(self.unit):
                tile, off = (q * self.Sp) // LANES, (q * self.Sp) % LANES
                for first in range(0, self.n_s, share):
                    total = None
                    for b in range(first, min(first + share, self.n_s)):
                        turn = ((b - first) * self.Sp - off) % LANES
                        value = got[ks, b, :, tile * LANES : (tile + 1) * LANES]
                        if turn:
                            value = pltpu.roll(value, turn, 1)
                        total = value if total is None else jnp.where(lane == b - first, value, total)
                    where = first * self.Sp
                    width = min(LANES, self.keys - where)
                    spot = ks * self.unit + q
                    for h in range(heads):
                        bias[h, spot : spot + 1, where : where + width] += total[h : h + 1, :width]

    def wait_sends(self, refs):
        _, buf, _, _, _, send, _, _, _ = refs
        mine = lax.axis_index(self.s_axis)
        for chunk in range(self.chunks):
            rows = pl.ds(chunk * self.rows, self.rows)
            spot = buf.at[mine, rows]
            for step in range(1, self.n_s):
                pltpu.make_async_copy(spot, spot, send.at[chunk, step]).wait()
        self.bias_copies(refs, False)

    def attend(self, refs, in_w, out_w, maskrow, consume):
        x, buf, _, _, bias, _, _, _, _ = refs
        heads, width = bias.shape[0], x.shape[-1]
        head_width = width // heads
        scale = head_width ** (-0.5)
        mine = lax.axis_index(self.s_axis)
        Sp, group = self.Sp, self.group
        which = lax.broadcasted_iota(jnp.int32, (heads, 1, width), 2) // head_width
        select = which == lax.broadcasted_iota(jnp.int32, (heads, 1, width), 0)
        select_f = select.astype(F32)

        def step(start):
            rows = pl.ds(start, group)
            normed = buf[:, rows].reshape(self.n_s * group * Sp, width)
            own = buf[mine, rows].reshape(group * Sp, width)
            keys = dot(normed, in_w[:, width : 2 * width]).astype(BF16)
            vals = dot(normed, in_w[:, 2 * width : 3 * width]).astype(BF16)
            keys = keys.reshape(self.n_s, group, Sp, width)
            vals = vals.reshape(self.n_s, group, Sp, width)
            query = dot(own, in_w[:, :width]).astype(BF16).astype(F32).reshape(group, Sp, width)
            gate = dot(own, in_w[:, 3 * width :]).astype(BF16).astype(F32)
            table = bias[...].reshape(heads * Sp, self.keys)
            hidden = maskrow[...]
            mixed = []
            for r in range(group):
                split = (query[r][None] * select_f).astype(BF16).reshape(heads * Sp, width)
                scores = dot_t(split, keys[:, r].reshape(self.keys, width)) * scale
                scores = (scores + table) + hidden
                top = jnp.max(scores, axis=-1, keepdims=True)
                weights = jnp.exp(scores - top)
                norm = jnp.sum(weights, axis=-1, keepdims=True)
                probs = (weights * (1.0 / norm)).astype(BF16)
                out = dot(probs, vals[:, r].reshape(self.keys, width)).reshape(heads, Sp, width)
                mixed.append(jnp.sum(jnp.where(select, out, 0.0), axis=0))
            mixed = mixed[0] if group == 1 else jnp.concatenate(mixed, axis=0)
            gated = (jax.nn.sigmoid(gate) * mixed).astype(BF16)
            old = x[rows].reshape(group * Sp, width)
            consume(start, (old + dot(gated, out_w[...])).astype(BF16).astype(F32))

        @pl.loop(0, self.chunks)
        def _(chunk):
            self.wait_rows(refs, chunk)

            @pl.loop(0, self.rows // group)
            def _(index):
                step(chunk * self.rows + index * group)


def kernel(phases, sizes, pair, extra0, extra1, mask0, mask1, in_w, out_w, bias_w, up, down, result, *scratch):
    n_gr, n_gc = sizes
    one, two = phases
    refs1, refs2 = scratch[:9], scratch[9:18]
    middle, ending = scratch[18:]
    x1, x2 = refs1[0], refs2[0]
    gr, gc = lax.axis_index("gr"), lax.axis_index("gc")
    barrier = pltpu.get_barrier_semaphore()
    for dr in range(n_gr):
        for dc in range(n_gc):
            if dr or dc:
                peer = {"gr": lax.rem(gr + dr, n_gr), "gc": lax.rem(gc + dc, n_gc)}
                pl.semaphore_signal(barrier, inc=1, device_id=peer, device_id_type=MESH)
    x1[...] = jnp.zeros_like(x1)
    x2[...] = jnp.zeros_like(x2)
    x1[:, : one.S, :] = pair[...].astype(F32)
    pl.semaphore_wait(barrier, n_gr * n_gc - 1)
    for chunk in range(one.chunks):
        one.send_rows(refs1, chunk)
    one.send_bias(refs1, bias_w[0])
    one.finish_bias(refs1, extra0)

    def transition(start, first):
        hidden = jnp.maximum(dot(layer_norm(first), up[...]), 0.0).astype(BF16)
        second = (first + dot(hidden, down[...])).astype(BF16).astype(F32)
        middle[pl.ds(pl.multiple_of(start * one.Sp, 8), one.group * one.Sp), :] = second

    one.attend(refs1, in_w.at[0], out_w.at[0], mask0, transition)
    for column in range(two.P):
        x2[column, : two.S, :] = middle[pl.ds(column, two.S, stride=one.Sp), :]
    for chunk in range(two.chunks):
        two.send_rows(refs2, chunk)
    two.send_bias(refs2, bias_w[1])
    two.finish_bias(refs2, extra1)

    def keep(start, final):
        ending[pl.ds(pl.multiple_of(start * two.Sp, 8), two.group * two.Sp), :] = final

    two.attend(refs2, in_w.at[1], out_w.at[1], mask1, keep)
    for row in range(one.P):
        result[row] = ending[pl.ds(row, one.S, stride=two.Sp), :].astype(BF16)
    one.wait_sends(refs1)
    two.wait_sends(refs2)


def key_row(values, phase, fill):
    values = values.reshape(phase.n_s, phase.S)
    values = jnp.pad(values, ((0, 0), (0, phase.Sp - phase.S)), constant_values=fill)
    return values.reshape(1, phase.keys)


def chain_term(chain_ids, weights, phase):
    own = lax.dynamic_slice_in_dim(chain_ids, lax.axis_index(phase.s_axis) * phase.S, phase.S)
    own = jnp.pad(own, (0, phase.Sp - phase.S), constant_values=-1)
    same = (own[:, None] == key_row(chain_ids, phase, -2)).astype(F32)
    return weights[:, None, None] * same[None]


def per_device(phases, sizes, pair, mask, chain_ids, attn_in, attn_out, bias_weight, chain_bias, trans_up, trans_down):
    one, two = phases
    width, heads = bias_weight.shape[1:]
    maskadd = jnp.where(mask > 0, 0.0, -1000000000.0).astype(F32)
    extras = [chain_term(chain_ids, chain_bias[a], phase) for a, phase in enumerate(phases)]
    masks = [key_row(maskadd, phase, PADDED) for phase in phases]
    bias_t = jnp.pad(jnp.transpose(bias_weight, (0, 2, 1)), ((0, 0), (0, 16 - heads), (0, 0)))
    vmem = pl.BlockSpec(memory_space=pltpu.VMEM)
    return pl.pallas_call(
        functools.partial(kernel, phases, sizes),
        out_shape=jax.ShapeDtypeStruct(pair.shape, BF16),
        in_specs=[vmem] * 10,
        out_specs=vmem,
        scratch_shapes=[
            *one.scratch(heads, width),
            *two.scratch(heads, width),
            pltpu.VMEM((one.P * one.Sp, width), F32),
            pltpu.VMEM((two.P * two.Sp, width), F32),
        ],
        compiler_params=pltpu.CompilerParams(
            collective_id=0, has_side_effects=True, vmem_limit_bytes=60 * 2**20
        ),
    )(pair, *extras, *masks, attn_in, attn_out, bias_t, trans_up, trans_down)


def solution(mesh):
    sizes = (mesh.shape["gr"], mesh.shape["gc"])
    jobs = mesh.shape["jobs"]

    def whole(pair, *others):
        rows, columns = pair.shape[0] // (jobs * sizes[0]), pair.shape[1] // sizes[1]
        chunks = 4
        while rows % chunks or columns % chunks:
            chunks -= 1
        phases = (
            Phase(rows, columns, sizes[0], sizes[1], "gr", "gc", chunks),
            Phase(columns, rows, sizes[1], sizes[0], "gc", "gr", chunks),
        )
        in_specs = (P(("jobs", "gr"), "gc", None), P("jobs"), P("jobs"), P(), P(), P(), P(), P(), P())
        return jax.shard_map(
            functools.partial(per_device, phases, sizes),
            mesh=mesh,
            in_specs=in_specs,
            out_specs=P(("jobs", "gr"), "gc", None),
            check_vma=False,
        )(pair, *others)

    return whole
```

time: 100 us -> 63.4 us (0.63)
  blocking collectives: 58.1 us -> 0 us
  Pallas kernels: 0 us -> 56.7 us
  starting transfers between devices: 13.1 us -> 0 us
  waiting for transfers between devices: 9.75 us -> 0 us
  matrix products: 5.86 us -> 0 us
  local copies, waits for them, and re-layouts: 8.6 us -> 5.68 us
  other arithmetic: 3.36 us -> 0.81 us
    pallas_call x0 -> x1, Pallas kernels: none -> 56.7 us  [per_device(): pl.pallas_call(functools.partial(kernel, phases, sizes), out_shape=jax.Sh...]
    all_gather x3 -> x0, blocking collectives: 50.3 us -> none  [the longest x1 31.1 us: per_device(): lax.all_gather(jnp.transpose(start_part, (2, 0, 1)), ('gr', 'gc'), axis=1...]
    all_to_all x3 -> x0, starting transfers between devices: 13.1 us -> none  [the longest x1 6.45 us: per_device(): rows = lax.all_to_all(pair, 'gc', split_axis=0, concat_axis=1, tiled=True)]
    all_to_all x3 -> x0, waiting for transfers between devices: 9.75 us -> none  [the longest x1 5.9 us: per_device(): tile = lax.all_to_all(rows, 'gc', split_axis=1, concat_axis=0, tiled=True)]
    all_to_all x1 -> x0, blocking collectives: 7.86 us -> none  [per_device(): lax.all_to_all(columns, 'gr', split_axis=1, concat_axis=0, tiled=True)]
    dot_general x27 -> x0, matrix products: 5.86 us -> none  [the longest x10 2.2 us: one_row(): jnp.einsum('jhd,khd->hjk', query, keys, preferred_element_type=jnp.float32)]
    reduce_sum x7 -> x0, other arithmetic: 1.43 us -> none  [the longest x4 1 us: layer_norm(): spread = jnp.mean((floats - center) ** 2, axis=-1, keepdims=True)]
    dynamic_slice x22 -> x1, local copies, waits for them, and re-layouts: 1.45 us -> 0.08 us  [chain_term(): lax.dynamic_slice_in_dim(chain_ids, lax.axis_index(phase.s_axis) * phase....]
  transfers between devices with their start and end apart: 3 -> 0, of which waited for: 2 -> 0; matrix products, arithmetic and copies ran while one was open for 1% -> 0% of each run, Pallas kernels for 0% -> 0%
where the time goes in v1:
time: 63.4 us; the launch traced here: 63.2 us
  Pallas kernels  56.7 us (89%)
  local copies, waits for them, and re-layouts  5.68 us (9%)
  other arithmetic  0.81 us (1%)
    pallas_call x1, Pallas kernels, per_device(): pl.pallas_call(functools.partial(kernel, phases, sizes), out_shape=jax.Sh...  56.7 us
    unnamed x9, local copies, waits for them, and re-layouts  4.14 us

profile of v1, /device:TPU:0, one launch (start us, length us, event | category | flops | bytes accessed | tf_op | source)
XLA Modules:
  0.0 63.2 jit_solution(3536105884804673661)
XLA Ops:
  0.0 0.0 copy-start
  0.0 0.7 %copy-done = s32[80]{0:T(128)S(1)} copy-done((s32[80]{0:T(128)S(1)}, s32[80]{0:T(128)}, u32[]{:S(2)}) %copy-start) | copy-done | bytes 344
  0.7 0.1 fusion
  0.7 0.0 copy-start.3
  0.7 0.6 %copy-done.3 = s32[80]{0:T(128)S(1)} copy-done((s32[80]{0:T(128)S(1)}, s32[80]{0:T(128)}, u32[]{:S(2)}) %copy-start.3) | copy-done | bytes 344
  1.4 0.0 copy-start.2
  1.4 0.7 %copy-done.2 = f32[2,4]{1,0:T(2,128)S(1)} copy-done((f32[2,4]{1,0:T(2,128)S(1)}, f32[2,4]{1,0:T(2,128)}, u32[]{:S(2)}) %copy-start.2) | copy-done | bytes 56
  2.1 0.1 reshape.78
  2.2 0.6 reshape.79.mask0.mask1
  2.8 0.1 reshape.77
  2.9 0.0 copy-start.1
  2.9 0.1 eq.35
  2.9 0.6 copy-done.1
  3.5 0.6 pad.25.bias_w
  4.1 0.1 compare_convert_fusion
  4.2 0.7 %broadcast_multiply_fusion = (f32[4,32,128]{2,1,0:T(8,128)}, f32[4,32,128]{2,1,0:T(8,128)}) fusion(f32[32,128]{1,0:T(8,128)S(1)} %get-tuple-element.7, f32[4]{0:T(128)S(1)} %get-tuple-element.5, f32[32,128]{1,0:T(8,128)S(1)} %get-tuple-element.8, f32[4]{0:T(128)S(1)} %get-tuple-element.6), kind=kLoop, calls=%fused_computation | loop fusion | flops 32768 | bytes 163872 | tf_op jit(solution)/shard_map/mul | solution.py:273
  4.9 56.7 %shard_map.91 = bf16[20,20,128]{2,1,0:T(8,128)(2,1)} custom-call(bf16[20,20,128]{2,1,0:T(8,128)(2,1)} %pair.1, f32[4,32,128]{2,1,0:T(8,128)} %get-tuple-element.12.extra0, f32[4,32,128]{2,1,0:T(8,128)} %get-tuple-element.11.extra1, f32[1,128]{1,0:T(1,128)} %reshape.79.mask0.mask1, f32[1,128]{1,0:T(1,128)} %reshape.79.mask0.mask1, bf16[2,128,512]{2,1,0:T(8,128)(2,1)} %in_w.1, ...), custom_call_target="tpu_custom_call" | custom-call | tf_op jit(solution)/shard_map/pallas_call | solution.py:284
  61.7 1.6 %copy.11 = bf16[20,20,128]{2,1,0:T(8,128)(2,1)} copy(bf16[20,20,128]{2,1,0:T(8,128)(2,1)} %shard_map.91) | data formatting | bytes 204800
  (6 shorter events, 0.0 us)
Async XLA Ops:
  0.0 0.7 %copy-start = (s32[80]{0:T(128)S(1)}, s32[80]{0:T(128)}, u32[]{:S(2)}) copy-start(s32[80]{0:T(128)} %param.11) | copy-start | bytes 964
  0.7 0.7 %copy-start.3 = (s32[80]{0:T(128)S(1)}, s32[80]{0:T(128)}, u32[]{:S(2)}) copy-start(s32[80]{0:T(128)} %param.10) | copy-start | bytes 964
  1.4 0.7 %copy-start.2 = (f32[2,4]{1,0:T(2,128)S(1)}, f32[2,4]{1,0:T(2,128)}, u32[]{:S(2)}) copy-start(f32[2,4]{1,0:T(2,128)} %param.15) | copy-start | bytes 100
  2.9 0.7 %copy-start.1 = (bf16[2,128,4]{1,2,0:T(4,128)(2,1)S(1)}, bf16[2,128,4]{1,2,0:T(4,128)(2,1)}, u32[]{:S(2)}) copy-start(bf16[2,128,4]{1,2,0:T(4,128)(2,1)} %param.14) | copy-start | bytes 6148

commit v2 on v1

v2 whole, which is shorter than its diff:
```python
import functools

import jax
import jax.numpy as jnp
from jax import lax
from jax.experimental import pallas as pl
from jax.experimental.pallas import tpu as pltpu
from jax.sharding import PartitionSpec as P

F32 = jnp.float32
BF16 = jnp.bfloat16
MESH = pl.DeviceIdType.MESH
LANES = 128
PADDED = -3e38


def padded_size(size):
    width = 16
    while width < size:
        width *= 2
    return width


def layer_norm(floats):
    center = jnp.mean(floats, axis=-1, keepdims=True)
    moved = floats - center
    spread = jnp.mean(moved * moved, axis=-1, keepdims=True)
    return (moved * lax.rsqrt(spread + 1e-05)).astype(BF16)


def dot(left, right):
    return jnp.dot(left, right, preferred_element_type=F32)


def dot_t(left, right):
    return lax.dot_general(left, right, (((1,), (1,)), ((), ())), preferred_element_type=F32)


class Phase:
    def __init__(self, count, width, n_p, n_s, p_axis, s_axis, chunks):
        self.P, self.S, self.Sp = count, width, padded_size(width)
        self.n_p, self.n_s, self.p_axis, self.s_axis = n_p, n_s, p_axis, s_axis
        self.unit = min(count, width)
        self.chunks = chunks
        self.rows = count // chunks
        self.keys = n_s * self.Sp
        group = max(1, 640 // self.keys)
        while self.rows % group:
            group -= 1
        self.group = group

    def scratch(self, heads, width):
        return [
            pltpu.VMEM((self.P * self.S + self.Sp, width), F32),
            pltpu.VMEM((self.n_s, self.P * self.S, width), BF16),
            pltpu.VMEM((self.P // self.unit, heads, self.unit * self.Sp), F32),
            pltpu.VMEM((self.S // self.unit, self.n_s, heads, self.unit * self.Sp), F32),
            pltpu.VMEM((heads, self.Sp, self.keys), F32),
            pltpu.SemaphoreType.DMA((self.chunks, self.n_s)),
            pltpu.SemaphoreType.DMA((self.chunks, self.n_s)),
            pltpu.SemaphoreType.DMA((self.P // self.unit, self.n_p)),
            pltpu.SemaphoreType.DMA((self.S // self.unit, self.n_s)),
            pltpu.VMEM((self.n_s, self.rows * self.S + self.Sp, width), F32),
            pltpu.VMEM((self.P * self.S + self.Sp, width), F32),
            pltpu.VMEM((8, self.keys), F32),
        ]

    def span(self, chunk):
        size = self.rows * self.S
        return pl.ds(pl.multiple_of(chunk * size, 16), size)

    def norm_rows(self, refs, chunk):
        x, buf = refs[:2]
        own = refs[10]
        rows = self.span(chunk)
        normed = layer_norm(x[rows])
        own[rows] = normed.astype(F32)
        buf[lax.axis_index(self.s_axis), rows] = normed

    def padded(self, tokens):
        row = lax.broadcasted_iota(jnp.int32, tokens.shape, 0)
        return jnp.where(row < self.S, tokens, 0.0).astype(BF16)

    def key_row(self, refs, values, fill):
        base = refs[11]
        base[...] = jnp.zeros_like(base)
        base[:, : self.n_s * self.S] = jnp.broadcast_to(values.astype(F32), (8, self.n_s * self.S))
        plain = base[...]
        lane = lax.broadcasted_iota(jnp.int32, plain.shape, 1)
        row = plain
        for b in range(1, self.n_s):
            turned = pltpu.roll(plain, (b * (self.Sp - self.S)) % self.keys, 1)
            row = jnp.where(lane // self.Sp == b, turned, row)
        return plain, jnp.where(lane % self.Sp < self.S, row, fill)

    def chain_row(self, refs, bias, weights, chain_ids):
        plain, row = self.key_row(refs, chain_ids, -2.0)
        shape = (self.Sp, self.keys)
        lane = lax.broadcasted_iota(jnp.int32, shape, 1)
        spot = lax.broadcasted_iota(jnp.int32, shape, 0) + lax.axis_index(self.s_axis) * self.S
        own = jnp.sum(jnp.where(lane == spot, plain[:1], 0.0), axis=-1, keepdims=True)
        same = jnp.where(own == row[:1], 1.0, 0.0)
        for h in range(bias.shape[0]):
            bias[h] = weights(h) * same

    def device(self, p_index, s_index):
        return {self.p_axis: p_index, self.s_axis: s_index}

    def send_rows(self, refs, chunk):
        x, buf, _, _, _, send, recv = refs[:7]
        mine = lax.axis_index(self.s_axis)
        rows = self.span(chunk)
        for step in range(1, self.n_s):
            peer = lax.rem(mine + step, self.n_s)
            pltpu.make_async_remote_copy(
                src_ref=buf.at[mine, rows],
                dst_ref=buf.at[mine, rows],
                send_sem=send.at[chunk, step],
                recv_sem=recv.at[chunk, mine],
                device_id=self.device(lax.axis_index(self.p_axis), peer),
                device_id_type=MESH,
            ).start()

    def wait_rows(self, refs, chunk):
        _, buf, _, _, _, _, recv = refs[:7]
        mine = lax.axis_index(self.s_axis)
        rows = self.span(chunk)
        for step in range(1, self.n_s):
            peer = lax.rem(mine + step, self.n_s)
            spot = buf.at[peer, rows]
            pltpu.make_async_copy(spot, spot, recv.at[chunk, peer]).wait()

    def piece(self, k):
        start = lax.axis_index(self.p_axis) * self.P + k * self.unit
        return start // self.S, lax.rem(start, self.S) // self.unit

    def bias_copies(self, refs, begin):
        _, _, part, got, _, _, _, send, recv = refs[:9]
        mine_p, mine_s = lax.axis_index(self.p_axis), lax.axis_index(self.s_axis)
        for k in range(self.P // self.unit):
            target, slot = self.piece(k)
            for step in range(self.n_p):
                row = lax.rem(mine_p + step, self.n_p)
                copy = pltpu.make_async_remote_copy(
                    src_ref=part.at[k],
                    dst_ref=got.at[slot, mine_s],
                    send_sem=send.at[k, step],
                    recv_sem=recv.at[slot, mine_s],
                    device_id=self.device(row, target),
                    device_id_type=MESH,
                )
                act = copy.start if begin else copy.wait_send
                if step > 0:
                    act()
                    continue
                pl.when(target != mine_s)(act)
                if begin:

                    @pl.when(target == mine_s)
                    def _():
                        pltpu.make_async_copy(
                            part.at[k], got.at[slot, mine_s], recv.at[slot, mine_s]
                        ).start()

    def send_bias(self, refs, weight):
        part, tokens = refs[2], refs[10]
        for k in range(self.P // self.unit):
            starts = [(k * self.unit + q) * self.S for q in range(self.unit)]
            own = [self.padded(tokens[at : at + self.Sp]) for at in starts]
            part[k] = dot_t(weight, jnp.concatenate(own, axis=0))
        self.bias_copies(refs, True)

    def finish_bias(self, refs):
        _, _, _, got, bias, _, _, _, recv = refs[:9]
        heads = bias.shape[0]
        share = max(1, LANES // self.Sp)
        for ks in range(self.S // self.unit):
            for b in range(self.n_s):
                spot = got.at[ks, b]
                pltpu.make_async_copy(spot, spot, recv.at[ks, b]).wait()
        lane = lax.broadcasted_iota(jnp.int32, (heads, LANES), 1) // min(self.Sp, LANES)
        for ks in range(self.S // self.unit):
            for q in range(self.unit):
                tile, off = (q * self.Sp) // LANES, (q * self.Sp) % LANES
                for first in range(0, self.n_s, share):
                    total = None
                    for b in range(first, min(first + share, self.n_s)):
                        turn = ((b - first) * self.Sp - off) % LANES
                        value = got[ks, b, :, tile * LANES : (tile + 1) * LANES]
                        if turn:
                            value = pltpu.roll(value, turn, 1)
                        total = value if total is None else jnp.where(lane == b - first, value, total)
                    where = first * self.Sp
                    width = min(LANES, self.keys - where)
                    spot = ks * self.unit + q
                    for h in range(heads):
                        bias[h, spot : spot + 1, where : where + width] += total[h : h + 1, :width]

    def wait_sends(self, refs):
        _, buf, _, _, _, send = refs[:6]
        mine = lax.axis_index(self.s_axis)
        for chunk in range(self.chunks):
            rows = self.span(chunk)
            spot = buf.at[mine, rows]
            for step in range(1, self.n_s):
                pltpu.make_async_copy(spot, spot, send.at[chunk, step]).wait()
        self.bias_copies(refs, False)

    def attend(self, refs, in_w, out_w, maskrow, consume):
        x, buf, _, _, bias = refs[:5]
        stage = refs[9]
        heads, width = bias.shape[0], x.shape[-1]
        head_width = width // heads
        scale = head_width ** (-0.5)
        mine = lax.axis_index(self.s_axis)
        Sp, group = self.Sp, self.group
        which = lax.broadcasted_iota(jnp.int32, (heads, 1, width), 2) // head_width
        select = which == lax.broadcasted_iota(jnp.int32, (heads, 1, width), 0)
        select_f = select.astype(F32)

        def step(chunk, index):
            local = index * (group * self.S)
            places = [local + r * self.S for r in range(group)]
            normed = [
                self.padded(stage[b, pl.ds(at, Sp)]) for at in places for b in range(self.n_s)
            ]
            normed = jnp.concatenate(normed, axis=0)
            own = jnp.concatenate([self.padded(stage[mine, pl.ds(at, Sp)]) for at in places], axis=0)
            keys = dot(normed, in_w[:, width : 2 * width]).astype(BF16)
            vals = dot(normed, in_w[:, 2 * width : 3 * width]).astype(BF16)
            keys = keys.reshape(group, self.keys, width)
            vals = vals.reshape(group, self.keys, width)
            query = dot(own, in_w[:, :width]).astype(BF16).astype(F32).reshape(group, Sp, width)
            gate = dot(own, in_w[:, 3 * width :]).astype(BF16).astype(F32)
            table = bias[...].reshape(heads * Sp, self.keys)
            hidden = maskrow[:1]
            mixed = []
            for r in range(group):
                split = (query[r][None] * select_f).astype(BF16).reshape(heads * Sp, width)
                scores = dot_t(split, keys[r]) * scale
                scores = (scores + table) + hidden
                top = jnp.max(scores, axis=-1, keepdims=True)
                weights = jnp.exp(scores - top)
                norm = jnp.sum(weights, axis=-1, keepdims=True)
                probs = (weights * (1.0 / norm)).astype(BF16)
                out = dot(probs, vals[r]).reshape(heads, Sp, width)
                mixed.append(jnp.sum(jnp.where(select, out, 0.0), axis=0))
            mixed = mixed[0] if group == 1 else jnp.concatenate(mixed, axis=0)
            gated = (jax.nn.sigmoid(gate) * mixed).astype(BF16)
            begin = chunk * (self.rows * self.S)
            old = jnp.concatenate([x[pl.ds(begin + at, Sp)] for at in places], axis=0)
            consume(chunk * self.rows + index * group, (old + dot(gated, out_w[...])).astype(BF16).astype(F32))

        @pl.loop(0, self.chunks)
        def _(chunk):
            self.wait_rows(refs, chunk)
            for b in range(self.n_s):
                stage[b, : self.rows * self.S] = buf[b, self.span(chunk)].astype(F32)
            if self.rows == group:
                step(chunk, 0)
            else:
                pl.loop(0, self.rows // group)(lambda index: step(chunk, index))


def send_all(phase, refs, weight):
    phase.norm_rows(refs, 0)
    phase.send_rows(refs, 0)
    for chunk in range(1, phase.chunks):
        phase.norm_rows(refs, chunk)
    phase.send_bias(refs, weight)
    for chunk in range(1, phase.chunks):
        phase.send_rows(refs, chunk)


def kernel(phases, sizes, pair, mask, chain_ids, chain_w, in_w, out_w, bias_w, up, down, result, *scratch):
    n_gr, n_gc = sizes
    one, two = phases
    refs1, refs2 = scratch[:12], scratch[12:24]
    middle, ending, mask1, mask2 = scratch[24:]
    x1, x2 = refs1[0], refs2[0]
    gr, gc = lax.axis_index("gr"), lax.axis_index("gc")
    barrier = pltpu.get_barrier_semaphore()
    for dr in range(n_gr):
        for dc in range(n_gc):
            if dr or dc:
                peer = {"gr": lax.rem(gr + dr, n_gr), "gc": lax.rem(gc + dc, n_gc)}
                pl.semaphore_signal(barrier, inc=1, device_id=peer, device_id_type=MESH)
    for phase, refs in ((one, refs1), (two, refs2)):
        for ref, used in ((refs[0], phase.P * phase.S), (refs[10], phase.P * phase.S)):
            ref[used:] = jnp.zeros((phase.Sp, ref.shape[-1]), F32)
        for b in range(phase.n_s):
            refs[9][b, phase.rows * phase.S :] = jnp.zeros((phase.Sp, x1.shape[-1]), F32)
    for row in range(one.P):
        x1[row * one.S : (row + 1) * one.S] = pair[row].astype(F32)
    maskadd = jnp.where(mask[...] > 0, 0.0, -1000000000.0).astype(F32)
    for a, phase, refs, hidden in ((0, one, refs1, mask1), (1, two, refs2, mask2)):
        phase.chain_row(refs, refs[4], lambda h, a=a: chain_w[a, h], chain_ids[...])
        hidden[...] = phase.key_row(refs, maskadd, PADDED)[1]
    pl.semaphore_wait(barrier, n_gr * n_gc - 1)
    send_all(one, refs1, bias_w[0])
    one.finish_bias(refs1)

    def transition(start, first):
        hidden = jnp.maximum(dot(layer_norm(first), up[...]), 0.0).astype(BF16)
        second = (first + dot(hidden, down[...])).astype(BF16).astype(F32)
        middle[pl.ds(pl.multiple_of(start * one.Sp, 8), one.group * one.Sp), :] = second

    one.attend(refs1, in_w.at[0], out_w.at[0], mask1, transition)
    for column in range(two.P):
        x2[column * two.S : (column + 1) * two.S] = middle[pl.ds(column, two.S, stride=one.Sp), :]
    send_all(two, refs2, bias_w[1])
    two.finish_bias(refs2)

    def keep(start, final):
        ending[pl.ds(pl.multiple_of(start * two.Sp, 8), two.group * two.Sp), :] = final

    two.attend(refs2, in_w.at[1], out_w.at[1], mask2, keep)
    for row in range(one.P):
        result[row] = ending[pl.ds(row, one.S, stride=two.Sp), :].astype(BF16)
    one.wait_sends(refs1)
    two.wait_sends(refs2)


def per_device(phases, sizes, pair, mask, chain_ids, attn_in, attn_out, bias_weight, chain_bias, trans_up, trans_down):
    one, two = phases
    width, heads = bias_weight.shape[1:]
    vmem = pl.BlockSpec(memory_space=pltpu.VMEM)
    smem = pl.BlockSpec(memory_space=pltpu.SMEM)
    return pl.pallas_call(
        functools.partial(kernel, phases, sizes),
        out_shape=jax.ShapeDtypeStruct(pair.shape, BF16),
        in_specs=[vmem] * 3 + [smem] + [vmem] * 5,
        out_specs=vmem,
        scratch_shapes=[
            *one.scratch(heads, width),
            *two.scratch(heads, width),
            pltpu.VMEM((one.P * one.Sp, width), F32),
            pltpu.VMEM((two.P * two.Sp, width), F32),
            pltpu.VMEM((8, one.keys), F32),
            pltpu.VMEM((8, two.keys), F32),
        ],
        compiler_params=pltpu.CompilerParams(
            collective_id=0, has_side_effects=True, vmem_limit_bytes=60 * 2**20
        ),
    )(
        pair,
        mask.reshape(1, -1),
        chain_ids.reshape(1, -1),
        chain_bias,
        attn_in,
        attn_out,
        jnp.transpose(bias_weight, (0, 2, 1)),
        trans_up,
        trans_down,
    )


def solution(mesh):
    sizes = (mesh.shape["gr"], mesh.shape["gc"])
    jobs = mesh.shape["jobs"]

    def whole(pair, *others):
        rows, columns = pair.shape[0] // (jobs * sizes[0]), pair.shape[1] // sizes[1]
        chunks = 5
        while rows % chunks or columns % chunks or (rows * columns // chunks) % 16:
            chunks -= 1
        phases = (
            Phase(rows, columns, sizes[0], sizes[1], "gr", "gc", chunks),
            Phase(columns, rows, sizes[1], sizes[0], "gc", "gr", chunks),
        )
        in_specs = (P(("jobs", "gr"), "gc", None), P("jobs"), P("jobs"), P(), P(), P(), P(), P(), P())
        return jax.shard_map(
            functools.partial(per_device, phases, sizes),
            mesh=mesh,
            in_specs=in_specs,
            out_specs=P(("jobs", "gr"), "gc", None),
            check_vma=False,
        )(pair, *others)

    return whole
```

time: 63.4 us -> 42.6 us (0.67)
  Pallas kernels: 56.7 us -> 40.9 us
  local copies, waits for them, and re-layouts: 5.68 us -> 1.56 us
  other arithmetic: 0.81 us -> 0 us
    pallas_call x1, Pallas kernels: 56.7 us -> 40.9 us  [per_device(): pl.pallas_call(functools.partial(kernel, phases, sizes), out_shape=jax.Sh...]
    unnamed x9 -> x1, local copies, waits for them, and re-layouts: 4.14 us -> 1.56 us
    reshape x3 -> x0, local copies, waits for them, and re-layouts: 0.76 us -> none  [the longest x1 0.6 us: key_row(): return values.reshape(1, phase.keys)]
    mul x1 -> x0, other arithmetic: 0.73 us -> none  [chain_term(): return weights[:, None, None] * same[None]]
where the time goes in v2:
time: 42.6 us; the launch traced here: 42.5 us
  Pallas kernels  40.9 us (96%)
  local copies, waits for them, and re-layouts  1.56 us (4%)
    pallas_call x1, Pallas kernels, per_device(): pl.pallas_call(functools.partial(kernel, phases, sizes), out_shape=jax.Sh...  40.9 us
    unnamed x1, local copies, waits for them, and re-layouts  1.56 us

profile of v2, /device:TPU:0, one launch (start us, length us, event | category | flops | bytes accessed | tf_op | source)
XLA Modules:
  0.0 42.5 jit_solution(1919708094548900577)
XLA Ops:
  0.0 40.9 %shard_map.91 = bf16[20,20,128]{2,1,0:T(8,128)(2,1)} custom-call(bf16[20,20,128]{2,1,0:T(8,128)(2,1)} %pair.1, s32[1,80]{1,0:T(1,128)} %bitcast.4, s32[1,80]{1,0:T(1,128)} %bitcast.5, f32[2,4]{1,0:T(2,128)} %chain_w.1, bf16[2,128,512]{2,1,0:T(8,128)(2,1)} %in_w.1, bf16[2,128,128]{2,1,0:T(8,128)(2,1)} %out_w.1, bf16[2,4,128]{2,1,0:T(4,128)(2,1)} %bitcast.3, ...), custom_call_target="tpu_custom_call" | custom-call | tf_op jit(solution)/shard_map/pallas_call | solution.py:329
  40.9 1.6 %copy.11 = bf16[20,20,128]{2,1,0:T(8,128)(2,1)} copy(bf16[20,20,128]{2,1,0:T(8,128)(2,1)} %shard_map.91) | data formatting | bytes 204800

commit v3 on v2

--- a/solution.py
+++ b/solution.py
@@ -12,6 +12,7 @@
 MESH = pl.DeviceIdType.MESH
 LANES = 128
 PADDED = -3e38
+BATCHES = ((0, 1), (2, 3, 4))
 
 
 def padded_size(size):
@@ -19,6 +20,10 @@
     while width < size:
         width *= 2
     return width
+
+
+def aligned(start):
+    return start if isinstance(start, int) else pl.multiple_of(start, 16)
 
 
 def layer_norm(floats):
@@ -48,6 +53,10 @@
         while self.rows % group:
             group -= 1
         self.group = group
+        self.batches = None
+        if group == self.rows and chunks == 5:
+            self.batches = BATCHES
+        self.staged = 1 if self.batches is None else max(len(b) for b in self.batches)
 
     def scratch(self, heads, width):
         return [
@@ -60,14 +69,14 @@
             pltpu.SemaphoreType.DMA((self.chunks, self.n_s)),
             pltpu.SemaphoreType.DMA((self.P // self.unit, self.n_p)),
             pltpu.SemaphoreType.DMA((self.S // self.unit, self.n_s)),
-            pltpu.VMEM((self.n_s, self.rows * self.S + self.Sp, width), F32),
+            pltpu.VMEM((self.n_s, self.staged * self.rows * self.S + self.Sp, width), F32),
             pltpu.VMEM((self.P * self.S + self.Sp, width), F32),
             pltpu.VMEM((8, self.keys), F32),
         ]
 
     def span(self, chunk):
         size = self.rows * self.S
-        return pl.ds(pl.multiple_of(chunk * size, 16), size)
+        return pl.ds(aligned(chunk * size), size)
 
     def norm_rows(self, refs, chunk):
         x, buf = refs[:2]
@@ -213,12 +222,12 @@
         head_width = width // heads
         scale = head_width ** (-0.5)
         mine = lax.axis_index(self.s_axis)
-        Sp, group = self.Sp, self.group
+        Sp = self.Sp
         which = lax.broadcasted_iota(jnp.int32, (heads, 1, width), 2) // head_width
         select = which == lax.broadcasted_iota(jnp.int32, (heads, 1, width), 0)
         select_f = select.astype(F32)
 
-        def step(chunk, index):
+        def step(chunk, index, group):
             local = index * (group * self.S)
             places = [local + r * self.S for r in range(group)]
             normed = [
@@ -230,6 +239,7 @@
             vals = dot(normed, in_w[:, 2 * width : 3 * width]).astype(BF16)
             keys = keys.reshape(group, self.keys, width)
             vals = vals.reshape(group, self.keys, width)
+            ones = jnp.ones((self.keys, width), BF16)
             query = dot(own, in_w[:, :width]).astype(BF16).astype(F32).reshape(group, Sp, width)
             gate = dot(own, in_w[:, 3 * width :]).astype(BF16).astype(F32)
             table = bias[...].reshape(heads * Sp, self.keys)
@@ -241,25 +251,34 @@
                 scores = (scores + table) + hidden
                 top = jnp.max(scores, axis=-1, keepdims=True)
                 weights = jnp.exp(scores - top)
-                norm = jnp.sum(weights, axis=-1, keepdims=True)
-                probs = (weights * (1.0 / norm)).astype(BF16)
-                out = dot(probs, vals[r]).reshape(heads, Sp, width)
-                mixed.append(jnp.sum(jnp.where(select, out, 0.0), axis=0))
+                both = dot(weights.astype(BF16), jnp.concatenate([vals[r], ones], axis=1))
+                both = both.reshape(heads, Sp, 2 * width)
+                total = jnp.sum(jnp.where(select, both[:, :, :width], 0.0), axis=0)
+                norm = jnp.sum(jnp.where(select, both[:, :, width:], 0.0), axis=0)
+                mixed.append(total / norm)
             mixed = mixed[0] if group == 1 else jnp.concatenate(mixed, axis=0)
             gated = (jax.nn.sigmoid(gate) * mixed).astype(BF16)
             begin = chunk * (self.rows * self.S)
             old = jnp.concatenate([x[pl.ds(begin + at, Sp)] for at in places], axis=0)
             consume(chunk * self.rows + index * group, (old + dot(gated, out_w[...])).astype(BF16).astype(F32))
 
+        def fetch(chunk, place):
+            self.wait_rows(refs, chunk)
+            size = self.rows * self.S
+            for b in range(self.n_s):
+                stage[b, place * size : (place + 1) * size] = buf[b, self.span(chunk)].astype(F32)
+
+        if self.batches is not None:
+            for batch in self.batches:
+                for place, chunk in enumerate(batch):
+                    fetch(chunk, place)
+                step(batch[0], 0, self.rows * len(batch))
+            return
+
         @pl.loop(0, self.chunks)
         def _(chunk):
-            self.wait_rows(refs, chunk)
-            for b in range(self.n_s):
-                stage[b, : self.rows * self.S] = buf[b, self.span(chunk)].astype(F32)
-            if self.rows == group:
-                step(chunk, 0)
-            else:
-                pl.loop(0, self.rows // group)(lambda index: step(chunk, index))
+            fetch(chunk, 0)
+            pl.loop(0, self.rows // self.group)(lambda index: step(chunk, index, self.group))
 
 
 def send_all(phase, refs, weight):
@@ -289,7 +308,7 @@
         for ref, used in ((refs[0], phase.P * phase.S), (refs[10], phase.P * phase.S)):
             ref[used:] = jnp.zeros((phase.Sp, ref.shape[-1]), F32)
         for b in range(phase.n_s):
-            refs[9][b, phase.rows * phase.S :] = jnp.zeros((phase.Sp, x1.shape[-1]), F32)
+            refs[9][b, phase.staged * phase.rows * phase.S :] = jnp.zeros((phase.Sp, x1.shape[-1]), F32)
     for row in range(one.P):
         x1[row * one.S : (row + 1) * one.S] = pair[row].astype(F32)
     maskadd = jnp.where(mask[...] > 0, 0.0, -1000000000.0).astype(F32)
@@ -303,7 +322,7 @@
     def transition(start, first):
         hidden = jnp.maximum(dot(layer_norm(first), up[...]), 0.0).astype(BF16)
         second = (first + dot(hidden, down[...])).astype(BF16).astype(F32)
-        middle[pl.ds(pl.multiple_of(start * one.Sp, 8), one.group * one.Sp), :] = second
+        middle[pl.ds(aligned(start * one.Sp), second.shape[0]), :] = second
 
     one.attend(refs1, in_w.at[0], out_w.at[0], mask1, transition)
     for column in range(two.P):
@@ -312,7 +331,7 @@
     two.finish_bias(refs2)
 
     def keep(start, final):
-        ending[pl.ds(pl.multiple_of(start * two.Sp, 8), two.group * two.Sp), :] = final
+        ending[pl.ds(aligned(start * two.Sp), final.shape[0]), :] = final
 
     two.attend(refs2, in_w.at[1], out_w.at[1], mask2, keep)
     for row in range(one.P):

time: 42.6 us -> 31 us (0.73)
  Pallas kernels: 40.9 us -> 29.3 us
    pallas_call x1, Pallas kernels: 40.9 us -> 29.3 us  [per_device(): pl.pallas_call(functools.partial(kernel, phases, sizes), out_shape=jax.Sh...]
where the time goes in v3:
time: 31 us; the launch traced here: 30.9 us
  Pallas kernels  29.3 us (95%)
  local copies, waits for them, and re-layouts  1.56 us (5%)
    pallas_call x1, Pallas kernels, per_device(): pl.pallas_call(functools.partial(kernel, phases, sizes), out_shape=jax.Sh...  29.3 us
    unnamed x1, local copies, waits for them, and re-layouts  1.56 us

profile of v3, /device:TPU:0, one launch (start us, length us, event | category | flops | bytes accessed | tf_op | source)
XLA Modules:
  0.0 30.9 jit_solution(11174222756878233302)
XLA Ops:
  0.0 29.3 %shard_map.91 = bf16[20,20,128]{2,1,0:T(8,128)(2,1)} custom-call(bf16[20,20,128]{2,1,0:T(8,128)(2,1)} %pair.1, s32[1,80]{1,0:T(1,128)} %bitcast.4, s32[1,80]{1,0:T(1,128)} %bitcast.5, f32[2,4]{1,0:T(2,128)} %chain_w.1, bf16[2,128,512]{2,1,0:T(8,128)(2,1)} %in_w.1, bf16[2,128,128]{2,1,0:T(8,128)(2,1)} %out_w.1, bf16[2,4,128]{2,1,0:T(4,128)(2,1)} %bitcast.3, ...), custom_call_target="tpu_custom_call" | custom-call | tf_op jit(solution)/shard_map/pallas_call | solution.py:348
  29.3 1.6 %copy.11 = bf16[20,20,128]{2,1,0:T(8,128)(2,1)} copy(bf16[20,20,128]{2,1,0:T(8,128)(2,1)} %shard_map.91) | data formatting | bytes 204800

commit v4 on v3

--- a/solution.py
+++ b/solution.py
@@ -12,7 +12,7 @@
 MESH = pl.DeviceIdType.MESH
 LANES = 128
 PADDED = -3e38
-BATCHES = ((0, 1), (2, 3, 4))
+BATCHES = {"gc": ((0,), (1, 2), (3, 4)), "gr": ((0, 1), (2, 3, 4))}
 
 
 def padded_size(size):
@@ -55,7 +55,7 @@
         self.group = group
         self.batches = None
         if group == self.rows and chunks == 5:
-            self.batches = BATCHES
+            self.batches = BATCHES[s_axis]
         self.staged = 1 if self.batches is None else max(len(b) for b in self.batches)
 
     def scratch(self, heads, width):
@@ -119,7 +119,7 @@
         x, buf, _, _, _, send, recv = refs[:7]
         mine = lax.axis_index(self.s_axis)
         rows = self.span(chunk)
-        for step in range(1, self.n_s):
+        for step in sorted(range(1, self.n_s), key=lambda step: -min(step, self.n_s - step)):
             peer = lax.rem(mine + step, self.n_s)
             pltpu.make_async_remote_copy(
                 src_ref=buf.at[mine, rows],
@@ -282,12 +282,10 @@
 
 
 def send_all(phase, refs, weight):
-    phase.norm_rows(refs, 0)
-    phase.send_rows(refs, 0)
-    for chunk in range(1, phase.chunks):
+    for chunk in range(phase.chunks):
         phase.norm_rows(refs, chunk)
     phase.send_bias(refs, weight)
-    for chunk in range(1, phase.chunks):
+    for chunk in range(phase.chunks):
         phase.send_rows(refs, chunk)
 
 

time: 31 us -> 30.5 us (0.984); the launches traced: 30.9 us -> 29.9 us
  Pallas kernels: 29.3 us -> 28.3 us
    pallas_call x1, Pallas kernels: 29.3 us -> 28.3 us  [per_device(): pl.pallas_call(functools.partial(kernel, phases, sizes), out_shape=jax.Sh...]
where the time goes in v4:
time: 30.5 us; the launch traced here: 29.9 us
  Pallas kernels  28.3 us (93%)
  local copies, waits for them, and re-layouts  1.56 us (5%)
    pallas_call x1, Pallas kernels, per_device(): pl.pallas_call(functools.partial(kernel, phases, sizes), out_shape=jax.Sh...  28.3 us
    unnamed x1, local copies, waits for them, and re-layouts  1.56 us

profile of v4, /device:TPU:0, one launch (start us, length us, event | category | flops | bytes accessed | tf_op | source)
XLA Modules:
  0.0 29.9 jit_solution(1795690419982713719)
XLA Ops:
  0.0 28.3 %shard_map.91 = bf16[20,20,128]{2,1,0:T(8,128)(2,1)} custom-call(bf16[20,20,128]{2,1,0:T(8,128)(2,1)} %pair.1, s32[1,80]{1,0:T(1,128)} %bitcast.4, s32[1,80]{1,0:T(1,128)} %bitcast.5, f32[2,4]{1,0:T(2,128)} %chain_w.1, bf16[2,128,512]{2,1,0:T(8,128)(2,1)} %in_w.1, bf16[2,128,128]{2,1,0:T(8,128)(2,1)} %out_w.1, bf16[2,4,128]{2,1,0:T(4,128)(2,1)} %bitcast.3, ...), custom_call_target="tpu_custom_call" | custom-call | tf_op jit(solution)/shard_map/pallas_call | solution.py:346
  28.3 1.6 %copy.11 = bf16[20,20,128]{2,1,0:T(8,128)(2,1)} copy(bf16[20,20,128]{2,1,0:T(8,128)(2,1)} %shard_map.91) | data formatting | bytes 204800
